TPU v7x, 32 devices: a whole 2x2x4 slice. The times are simulated.
32 devices in a mesh: grp: 4 (over y, x), blk: 8 (over z, core).
Axes of the slice: x: 2, y: 2, z: 4, core: 2. Of those that a mesh axis runs over, the one named last changes fastest.
Arguments:
- matrix: bfloat16 [8192, 8192], P('blk', 'grp')
- panels: bfloat16 [8192, 2048], P('grp', 'blk')
- pattern: int32 [64, 64], replicated, may hold values from 0 to 1, as said below
- pruned: int32 [64, 16], replicated, may hold values from 0 to 1, as said below
- owners: int32 [16], replicated, may hold values from 0 to 15, each once
Outputs:
- owned: float32 [8, 4, 256, 2048], P(None, 'grp', None, 'blk')
Inputs may be any that keep to these rules, and one draw needn't show every extreme that they name: `pattern`: 0 or 1; every diagonal block is 1. `pruned`: 0 or 1; block (c, c) is 1 for every window column block c; every block row holds exactly 8 ones. `owners`: each slot once.
All inputs are finite; a program needn't handle non-finite values.
Results may differ from a plain program's by a relative error of at most 0.0003.
Values may be sent and summed in bfloat16 or wider, within the bound.
A program may use at most 128 MiB of HBM per device.

v0:
```python
import jax
import jax.numpy as jnp
from jax import lax
from jax.sharding import PartitionSpec as P

BS = 128


def shards(matrix, panels, pattern, pruned, owners):
    blk_count = lax.axis_size("blk")
    blk_id = lax.axis_index("blk")
    grp_id = lax.axis_index("grp")
    row_count, inner = matrix.shape
    panel_width = panels.shape[1]
    row_blocks = row_count // BS
    inner_blocks = inner // BS
    panel_blocks = panel_width // BS
    width_total = panel_width * blk_count
    window_blocks = width_total // BS
    tile_left = lax.dynamic_slice(
        pattern, (blk_id * row_blocks, grp_id * inner_blocks), (row_blocks, inner_blocks)
    ).astype(jnp.bfloat16)
    left = (matrix.reshape(row_blocks, BS, inner_blocks, BS) * tile_left[:, None, :, None]).reshape(
        row_count, inner
    )
    tile_right = lax.dynamic_slice(
        pattern, (grp_id * inner_blocks, blk_id * panel_blocks), (inner_blocks, panel_blocks)
    ).astype(jnp.bfloat16)
    right = (
        panels.reshape(inner_blocks, BS, panel_blocks, BS) * tile_right[:, None, :, None]
    ).reshape(inner, panel_width)
    partial_value = jnp.dot(
        left, lax.all_gather(right, "blk", axis=1, tiled=True), preferred_element_type=jnp.float32
    )
    piece_rows = row_count // lax.axis_size("grp")
    first_row = blk_id * row_count + grp_id * piece_rows
    row_block = (first_row + jnp.arange(piece_rows, dtype=jnp.int32)) // BS
    select = (row_block[:, None] == jnp.arange(pattern.shape[0], dtype=jnp.int32)[None, :]).astype(
        jnp.float32
    )
    keep_mask = jnp.dot(select, pruned.astype(jnp.float32), precision=lax.Precision.HIGHEST)
    summed = lax.psum_scatter(partial_value, "grp", scatter_dimension=0, tiled=True)
    inflated = summed * summed
    kept = (inflated.reshape(piece_rows, window_blocks, BS) * keep_mask[:, :, None]).reshape(
        piece_rows, width_total
    )
    totals = lax.psum(jnp.sum(kept, axis=0), ("grp", "blk"))
    normalized = row_count * blk_count * kept / totals
    inverse = (
        jnp.zeros((window_blocks,), jnp.int32)
        .at[owners]
        .set(jnp.arange(window_blocks, dtype=jnp.int32))
    )
    arranged = normalized.reshape(piece_rows, window_blocks, BS)[:, inverse, :].reshape(
        1, piece_rows, width_total
    )
    moved = lax.all_to_all(arranged, "blk", split_axis=2, concat_axis=0, tiled=True)
    return moved[:, None, :, :]


def solution(mesh):
    in_specs = (P("blk", "grp"), P("grp", "blk"), P(), P(), P())
    out_specs = P(None, "grp", None, "blk")
    return jax.shard_map(shards, mesh=mesh, in_specs=in_specs, out_specs=out_specs, check_vma=False)
```

profile of v0, /device:TPU:25, one launch (start us, length us, event | category | flops | bytes accessed | tf_op | source)
XLA Modules:
  0.0 307.2 jit_solution(3839253676345963649)
XLA Ops:
  6.5 0.0 all-gather.2.cloned.1.call-start
  6.5 0.8 dynamic-slice_convert_fusion
  7.3 0.6 mul.64
  7.9 2.4 bitcast_multiply_fusion.3
  10.3 0.0 all-gather.2.cloned.1.call-update
  10.3 0.0 reduce-scatter.2.cloned.1.call-start
  10.4 0.8 dynamic-slice_convert_fusion.1
  11.2 81.1 %all-gather.2.cloned.1.call-done = bf16[2048,2048]{1,0:T(8,128)(2,1)} async-done(((bf16[2048,256]{1,0:T(8,128)(2,1)}), bf16[2048,2048]{1,0:T(8,128)(2,1)}) %all-gather.2.cloned.1.call-update) | async-done | bytes 8388624 | tf_op jit(solution)/shard_map/all_gather | solution.py:33
  92.3 0.0 copy-start.2
  92.3 0.6 mul.60
  92.9 1.6 copy-done.2
  94.4 13.2 %fusion = f32[1024,2048]{1,0:T(8,128)} fusion(bf16[2048,2048]{1,0:T(8,128)(2,1)} %all-gather.2.cloned.1.call-done, bf16[1024,2048]{1,0:T(8,128)(2,1)S(1)} %copy-done.2, bf16[128,8,16,128]{3,2,1,0:T(8,128)(2,1)S(1)} %bitcast.34), kind=kOutput, calls=%fused_computation.3 | convolution fusion | flops 8592031744 | bytes 25165824 | tf_op jit(solution)/shard_map/dot_general | solution.py:32
  107.6 0.0 copy-start.3
  107.6 0.0 copy-start.1
  107.6 0.0 reduce-scatter.2.cloned.1.call-update
  107.7 0.6 copy-done.3
  108.3 0.6 scatter_custom_fusion
  109.0 0.0 copy-done.1
  109.0 0.3 fusion.3
  109.3 84.9 %reduce-scatter.2.cloned.1.call-done = f32[256,2048]{1,0:T(8,128)} async-done(((f32[1024,2048]{1,0:T(8,128)}), f32[256,2048]{1,0:T(8,128)}) %reduce-scatter.2.cloned.1.call-update) | async-done | bytes 2097168 | tf_op jit(solution)/shard_map/reduce_scatter | solution.py:42
  194.1 0.0 copy-start
  194.1 0.6 mul.70
  194.7 1.0 copy-done
  195.7 1.1 fusion.2
  196.8 37.6 %psum.7 = f32[2048]{0:T(1024)S(1)} all-reduce(f32[2048]{0:T(1024)S(1)} %fusion.2), channel_id=1, replica_groups=mesh['grp'=4,'blk'=8] {'grp','blk'}, use_global_device_ids=true, to_apply=%region_2.3 | all-reduce | flops 2048 | bytes 16384 | tf_op jit(solution)/shard_map/psum | solution.py:47
  234.3 3.7 %copy_bitcast_fusion = f32[256,16,128]{2,0,1:T(8,128)} fusion(f32[2048]{0:T(1024)S(1)} %psum.7, f32[32,8,16,128]{3,2,1,0:T(8,128)S(1)} %bitcast.29, f32[256,2048]{1,0:T(8,128)} %reduce-scatter.2.cloned.1.call-done), kind=kLoop, calls=%fused_computation.6 | loop fusion | flops 2097152 | bytes 6299648 | tf_op jit(solution)/shard_map/reshape | solution.py:54
  238.0 2.3 gather_fusion
  240.3 1.8 copy.16
  242.1 3.8 %copy.17 = f32[1,256,2048]{1,0,2:T(1,128)S(1)} copy(f32[1,256,2048]{1,2,0:T(8,128)} %bitcast.31) | data formatting | bytes 4194304 | tf_op jit(solution)/shard_map/reshape | solution.py:54
  245.9 52.5 %all_to_all.15 = f32[1,256,2048]{1,0,2:T(1,128)S(1)} all-to-all(f32[1,256,2048]{1,0,2:T(1,128)S(1)} %copy.17), channel_id=1, replica_groups=mesh['grp'=4,'blk'=8] {'blk'}, dimensions={2} | all-to-all | bytes 4194304 | tf_op jit(solution)/shard_map/all_to_all | solution.py:57
  298.4 0.1 copy.20
  298.5 1.8 copy.18
  (5 shorter events, 0.0 us)
Async XLA Ops:
  6.5 85.7 %all-gather.2.cloned.1.call-start = ((), (), s32[]{:S(2)}) async-start(), calls=%async_computation.2 | async-start | bytes 9437184 | tf_op jit(solution)/shard_map/all_gather | solution.py:33
  10.3 183.8 %reduce-scatter.2.cloned.1.call-start = ((), (), s32[]{:S(2)}) async-start(), calls=%async_computation.3 | async-start | bytes 10485760 | tf_op jit(solution)/shard_map/reduce_scatter | solution.py:42
  92.3 2.2 copy-start.2
  107.6 0.7 copy-start.3
  107.6 1.3 copy-start.1
  194.1 1.6 copy-start
Sparse Core Ops, SparseCore 0:
  10.4 81.7 all-gather.1
  107.8 86.2 reduce-scatter.1
where the time goes:
time: 311 us; the launch traced here: 307 us
  waiting for transfers between devices  166 us (53%)
  blocking collectives  90 us (29%)
  local copies, waits for them, and re-layouts  15.4 us (5%)
  matrix products  13.5 us (4%)
  between operations  13.5 us (4%)
  other arithmetic  8.69 us (3%)
    reduce_scatter x1, waiting for transfers between devices, shards(): lax.psum_scatter(partial_value, 'grp', scatter_dimension=0, tiled=True)  84.9 us
    all_gather x1, waiting for transfers between devices, shards(): lax.all_gather(right, 'blk', axis=1, tiled=True)  81.1 us
    all_to_all x1, blocking collectives, shards(): lax.all_to_all(arranged, 'blk', split_axis=2, concat_axis=0, tiled=True)  52.5 us
    psum x1, blocking collectives, shards(): totals = lax.psum(jnp.sum(kept, axis=0), ('grp', 'blk'))  37.6 us
    dot_general x1, matrix products, shards(): jnp.dot(left, lax.all_gather(right, 'blk', axis=1, tiled=True), preferred...  13.2 us
  transfers between devices with their start and end apart: 2, of which 2 were waited for; matrix products, arithmetic and copies ran while one was open for 1% of the time, Pallas kernels for 0%

commit v1 on v0

v1 whole, which is shorter than its diff:
```python
import functools

import jax
import jax.numpy as jnp
from jax import lax
from jax.experimental import pallas as pl
from jax.experimental.pallas import tpu as pltpu
from jax.sharding import PartitionSpec as P

BS = 128
MESH = pl.DeviceIdType.MESH
CHUNKS = 4


def encode(values, ref, rows):
    ref[...] = values


def numbers(ref, rows):
    return ref[...]


def kernel(
    G, B,
    matrix_ref, panel_ref, pattern_ref, pruned_ref, owners_ref,
    out_ref, fac_ref,
    got_ref, own, left, pan, stage, rs, kept, out_stage, mine_tot, tot, inv,
    mat_sem, line_send, line_recv, sib_send, sib_recv, rs_send, rs_recv, out_send, out_recv, tot_send, tot_recv,
):
    grp = lax.axis_index("grp")
    blk = lax.axis_index("blk")
    M = B // 2
    m = lax.div(blk, 2)
    core = lax.rem(blk, 2)
    sib = m * 2 + (1 - core)
    rows, inner = left.shape
    width = panel_ref.shape[1]
    row_blocks, inner_blocks, panel_blocks = rows // BS, inner // BS, width // BS
    piece = rows // G
    piece_blocks = piece // BS
    chunk = inner // CHUNKS
    window_blocks = panel_blocks * B

    load = pltpu.make_async_copy(matrix_ref, left, mat_sem)
    load.start()

    barrier = pltpu.get_barrier_semaphore()

    def greet_blk(j, _):
        pl.semaphore_signal(barrier, inc=1, device_id={"blk": lax.rem(blk + j, B)}, device_id_type=MESH)
        return 0

    def greet_grp(j, _):
        pl.semaphore_signal(barrier, inc=1, device_id={"grp": lax.rem(grp + j, G)}, device_id_type=MESH)
        return 0

    lax.fori_loop(1, B, greet_blk, 0)
    lax.fori_loop(1, G, greet_grp, 0)
    pl.semaphore_wait(barrier, B - 1 + G - 1)

    def mask_panel(kb, _):
        at = pl.ds(pl.multiple_of(kb * BS, BS), BS)
        for cb in range(panel_blocks):
            keep = pattern_ref[grp * inner_blocks + kb, blk * panel_blocks + cb].astype(jnp.float32)
            cols = slice(cb * BS, (cb + 1) * BS)
            pan[blk, at, cols] = panel_ref[at, cols] * jnp.full((BS, BS), keep, jnp.float32).astype(jnp.bfloat16)
        return 0

    lax.fori_loop(0, inner_blocks, mask_panel, 0)

    def part(p, ch):
        return pan.at[p, pl.ds(pl.multiple_of(ch * chunk, chunk), chunk), :]

    def line_copy(src, ch, way):
        p = 2 * src + core
        to = blk + 2 - 4 * way
        return pltpu.make_async_remote_copy(
            src_ref=part(p, ch), dst_ref=part(p, ch),
            send_sem=line_send.at[way, src, ch], recv_sem=line_recv.at[src, ch],
            device_id={"blk": lax.rem(to + B, B)}, device_id_type=MESH,
        )

    def sib_copy(src, ch, c):
        p = 2 * src + c
        return pltpu.make_async_remote_copy(
            src_ref=part(p, ch), dst_ref=part(p, ch),
            send_sem=sib_send.at[src, ch], recv_sem=sib_recv.at[src, ch],
            device_id={"blk": sib}, device_id_type=MESH,
        )

    def rs_copy(p, i):
        return pltpu.make_async_remote_copy(
            src_ref=stage.at[p, i - 1], dst_ref=rs.at[p, i - 1],
            send_sem=rs_send.at[p, i - 1], recv_sem=rs_recv.at[p, i - 1],
            device_id={"grp": lax.rem(grp + i, G)}, device_id_type=MESH,
        )

    def send_own(ch, _):
        @pl.when(m + 1 < M)
        def _():
            line_copy(m, ch, 0).start()

        @pl.when(m > 0)
        def _():
            line_copy(m, ch, 1).start()

        sib_copy(m, ch, core).start()
        return 0

    lax.fori_loop(0, CHUNKS, send_own, 0)

    def invert(s, _):
        def look(c, best):
            return jnp.where(owners_ref[c] == s, c, best)

        inv[s] = lax.fori_loop(0, window_blocks, look, jnp.int32(0))
        return 0

    load.wait()

    def mask_left(rb, _):
        at = pl.ds(pl.multiple_of(rb * BS, BS), BS)
        for kb in range(inner_blocks):
            keep = pattern_ref[blk * row_blocks + rb, grp * inner_blocks + kb].astype(jnp.float32)
            cols = slice(kb * BS, (kb + 1) * BS)
            left[at, cols] = left[at, cols] * jnp.full((BS, BS), keep, jnp.float32).astype(jnp.bfloat16)
        return 0

    lax.fori_loop(0, row_blocks, mask_left, 0)

    def product(p, i):
        at = pl.ds(pl.multiple_of((lax.rem(grp + i, G)) * piece, piece), piece)
        return jnp.dot(left[at, :], pan[p], preferred_element_type=jnp.float32)

    def multiply(p):
        def for_peer(i, _):
            encode(product(p, i), stage.at[p, i - 1], piece)
            rs_copy(p, i).start()
            return 0

        for i in range(1, G):
            for_peer(i, 0)
        mine = product(p, 0)
        for cb in range(panel_blocks):
            kept[p * panel_blocks + cb] = mine[:, cb * BS : (cb + 1) * BS]

    def process(src):
        multiply(2 * src + core)

        def arrive(ch, _):
            sib_copy(src, ch, 1 - core).wait_recv()
            return 0

        lax.fori_loop(0, CHUNKS, arrive, 0)
        multiply(2 * src + 1 - core)

    def finish(src):
        def one(c, _):
            p = 2 * src + c

            def arrive(i, _):
                rs_copy(p, i).wait_recv()
                return 0

            for i in range(1, G):
                arrive(i, 0)
            total = jnp.concatenate([kept[p * panel_blocks + cb] for cb in range(panel_blocks)], axis=1)
            for i in range(1, G):
                message = rs.at[p, i - 1]
                total = total + numbers(message, piece)
            total = total * total
            for cb in range(panel_blocks):
                for rb in range(piece_blocks):
                    keep = pruned_ref[
                        blk * row_blocks + grp * piece_blocks + rb, p * panel_blocks + cb
                    ].astype(jnp.float32)
                    kept[p * panel_blocks + cb, rb * BS : (rb + 1) * BS, :] = (
                        total[rb * BS : (rb + 1) * BS, cb * BS : (cb + 1) * BS] * keep
                    )
            return 0

        lax.fori_loop(0, 2, one, 0)

    def pass_on(d):
        def one(ch, _):
            @pl.when(m - d >= 0)
            def _():
                line_copy(m - d, ch, 0).wait_recv()

                @pl.when(m + 1 < M)
                def _():
                    line_copy(m - d, ch, 0).start()

                sib_copy(m - d, ch, core).start()

            @pl.when(m + d < M)
            def _():
                line_copy(m + d, ch, 1).wait_recv()

                @pl.when(m > 0)
                def _():
                    line_copy(m + d, ch, 1).start()

                sib_copy(m + d, ch, core).start()

            return 0

        lax.fori_loop(0, CHUNKS, one, 0)

    def at_distance(d, work):
        @pl.when(m - d >= 0)
        def _():
            work(m - d)

        @pl.when(m + d < M)
        def _():
            work(m + d)

    process(m)
    lax.fori_loop(0, window_blocks, invert, 0)
    pass_on(1)
    finish(m)
    at_distance(1, process)

    def step(d, _):
        pass_on(d)
        at_distance(d - 1, finish)
        at_distance(d, process)
        return 0

    lax.fori_loop(2, M, step, 0)
    at_distance(M - 1, finish)

    def out_copy(j):
        return pltpu.make_async_remote_copy(
            src_ref=out_stage.at[j - 1], dst_ref=got_ref.at[j - 1],
            send_sem=out_send.at[j - 1], recv_sem=out_recv.at[j - 1],
            device_id={"blk": lax.rem(blk + j, B)}, device_id_type=MESH,
        )

    def in_slot_order(to, ref):
        encode(
            jnp.concatenate([kept[inv[to * panel_blocks + cb]] for cb in range(panel_blocks)], axis=1), ref, piece
        )

    def send_out(j, _):
        in_slot_order(lax.rem(blk + j, B), out_stage.at[j - 1])
        out_copy(j).start()
        return 0

    for j in range(1, B):
        send_out(j, 0)
    in_slot_order(blk, own)

    def add_up(source, message, total):
        values = numbers(message, piece)
        out_ref[source] = values
        return total + jnp.sum(values, axis=0, keepdims=True)

    total = add_up(blk, own, jnp.zeros((1, width), jnp.float32))
    for j in range(1, B):
        out_copy(j).wait_recv()
        total = add_up(lax.rem(blk + B - j, B), got_ref.at[j - 1], total)
    mine_tot[...] = jnp.broadcast_to(total, mine_tot.shape)

    def tot_copy(i):
        return pltpu.make_async_remote_copy(
            src_ref=mine_tot, dst_ref=tot.at[i - 1],
            send_sem=tot_send.at[i - 1], recv_sem=tot_recv.at[i - 1],
            device_id={"grp": lax.rem(grp + i, G)}, device_id_type=MESH,
        )

    for i in range(1, G):
        tot_copy(i).start()
    for i in range(1, G):
        tot_copy(i).wait_recv()
        total = total + tot[i - 1, 0:1, :]
    fac_ref[...] = jnp.broadcast_to(float(rows * B) / total, fac_ref.shape)

    for i in range(1, G):
        tot_copy(i).wait_send()

    def out_left(j, _):
        out_copy(j).wait_send()
        return 0

    for j in range(1, B):
        out_left(j, 0)

    def left_line(src, _):
        def one(ch, _):
            @pl.when((src <= m) & (m + 1 < M))
            def _():
                line_copy(src, ch, 0).wait_send()

            @pl.when((src >= m) & (m > 0))
            def _():
                line_copy(src, ch, 1).wait_send()

            sib_copy(src, ch, core).wait_send()
            return 0

        lax.fori_loop(0, CHUNKS, one, 0)
        return 0

    lax.fori_loop(0, M, left_line, 0)

    def left_rs(p, _):
        def one(i, _):
            rs_copy(p, i).wait_send()
            return 0

        for i in range(1, G):
            one(i, 0)
        return 0

    lax.fori_loop(0, B, left_rs, 0)


def shards(matrix, panels, pattern, pruned, owners):
    B = lax.axis_size("blk")
    G = lax.axis_size("grp")
    rows, inner = matrix.shape
    width = panels.shape[1]
    piece = rows // G
    window_blocks = width * B // BS
    M = B // 2
    dma = pltpu.SemaphoreType.DMA
    vmem = pl.BlockSpec(memory_space=pltpu.VMEM)
    smem = pl.BlockSpec(memory_space=pltpu.SMEM)
    got, fac = pl.pallas_call(
        functools.partial(kernel, G, B),
        out_shape=(
            jax.ShapeDtypeStruct((B, piece, width), jnp.float32),
            jax.ShapeDtypeStruct((8, width), jnp.float32),
        ),
        in_specs=[pl.BlockSpec(memory_space=pl.ANY), vmem, smem, smem, smem],
        out_specs=(vmem, vmem),
        scratch_shapes=[
            pltpu.VMEM((B - 1, piece, width), jnp.float32),
            pltpu.VMEM((piece, width), jnp.float32),
            pltpu.VMEM((rows, inner), jnp.bfloat16),
            pltpu.VMEM((B, inner, width), jnp.bfloat16),
            pltpu.VMEM((B, G - 1, piece, width), jnp.float32),
            pltpu.VMEM((B, G - 1, piece, width), jnp.float32),
            pltpu.VMEM((window_blocks, piece, BS), jnp.float32),
            pltpu.VMEM((B - 1, piece, width), jnp.float32),
            pltpu.VMEM((8, width), jnp.float32),
            pltpu.VMEM((G - 1, 8, width), jnp.float32),
            pltpu.SMEM((window_blocks,), jnp.int32),
            dma(()),
            dma((2, M, CHUNKS)),
            dma((M, CHUNKS)),
            dma((M, CHUNKS)),
            dma((M, CHUNKS)),
            dma((B, G - 1)),
            dma((B, G - 1)),
            dma((B - 1,)),
            dma((B - 1,)),
            dma((G - 1,)),
            dma((G - 1,)),
        ],
        compiler_params=pltpu.CompilerParams(
            collective_id=0, has_side_effects=True, vmem_limit_bytes=58 * 1024 * 1024
        ),
        cost_estimate=pl.CostEstimate(
            flops=2 * rows * inner * width * B, bytes_accessed=8 * 1024 * 1024, transcendentals=0
        ),
        name="expand",
    )(matrix, panels, pattern, pruned, owners)
    owned = got * fac[None, 0:1, :]
    return owned[:, None, :, :]


def solution(mesh):
    in_specs = (P("blk", "grp"), P("grp", "blk"), P(), P(), P())
    out_specs = P(None, "grp", None, "blk")
    return jax.shard_map(shards, mesh=mesh, in_specs=in_specs, out_specs=out_specs, check_vma=False)
```

time: 311 us -> 162 us (0.52); the launches traced: 307 us -> 162 us
  waiting for transfers between devices: 166 us -> 0 us
  Pallas kernels: 0 us -> 157 us
  blocking collectives: 90 us -> 0 us
  matrix products: 13.5 us -> 0 us
  between operations: 13.5 us -> 0.01 us
  local copies, waits for them, and re-layouts: 15.4 us -> 2.09 us
  other arithmetic: 8.69 us -> 3.12 us
    pallas_call x0 -> x1, Pallas kernels: none -> 157 us  [shards(): pl.pallas_call(functools.partial(kernel, G, B), out_shape=(jax.ShapeDtype...]
    reduce_scatter x1 -> x0, waiting for transfers between devices: 84.9 us -> none  [shards(): lax.psum_scatter(partial_value, 'grp', scatter_dimension=0, tiled=True)]
    all_gather x1 -> x0, waiting for transfers between devices: 81.1 us -> none  [shards(): lax.all_gather(right, 'blk', axis=1, tiled=True)]
    all_to_all x1 -> x0, blocking collectives: 52.5 us -> none  [shards(): lax.all_to_all(arranged, 'blk', split_axis=2, concat_axis=0, tiled=True)]
    psum x1 -> x0, blocking collectives: 37.6 us -> none  [shards(): totals = lax.psum(jnp.sum(kept, axis=0), ('grp', 'blk'))]
    dot_general x2 -> x0, matrix products: 13.5 us -> none  [the longest x1 13.2 us: shards(): jnp.dot(left, lax.all_gather(right, 'blk', axis=1, tiled=True), preferred...]
    gather x2 -> x0, local copies, waits for them, and re-layouts: 4.08 us -> none  [shards(): normalized.reshape(piece_rows, window_blocks, BS)[:, inverse, :]]
    reshape x1 -> x0, local copies, waits for them, and re-layouts: 3.78 us -> none  [shards(): normalized.reshape(piece_rows, window_blocks, BS)[:, inverse, :]]
  transfers between devices with their start and end apart: 2 -> 0, of which waited for: 2 -> 0; matrix products, arithmetic and copies ran while one was open for 1% -> 0% of each run, Pallas kernels for 0% -> 0%
where the time goes in v1:
time: 162 us
  Pallas kernels  157 us (97%)
  other arithmetic  3.12 us (2%)
  local copies, waits for them, and re-layouts  2.09 us (1%)
    pallas_call x1, Pallas kernels, shards(): pl.pallas_call(functools.partial(kernel, G, B), out_shape=(jax.ShapeDtype...  157 us

profile of v1, /device:TPU:25, one launch (start us, length us, event | category | flops | bytes accessed | tf_op | source)
XLA Modules:
  0.0 161.9 jit_solution(5574126970208361928)
XLA Ops:
  0.0 1.4 copy.6.pruned_ref
  1.4 156.7 %expand.1 = (f32[8,256,256]{2,1,0:T(8,128)}, f32[8,256]{1,0:T(8,128)}) custom-call(bf16[1024,2048]{1,0:T(8,128)(2,1)} %matrix_ref.1, bf16[2048,256]{1,0:T(8,128)(2,1)} %panel_ref.1, s32[64,64]{1,0:T(8,128)} %pattern_ref.1, s32[64,16]{1,0:T(8,128)} %copy.6.pruned_ref, s32[16]{0:T(128)} %owners_ref.1), custom_call_target="tpu_custom_call" | custom-call | flops 8589934592 | bytes 8388608 | tf_op jit(solution)/shard_map/expand/pallas_call | solution.py:331
  158.1 0.7 slice.3
  158.8 3.1 %multiply_bitcast_fusion = f32[8,1,256,256]{3,2,1,0:T(8,128)} fusion(f32[8,256,256]{2,1,0:T(8,128)} %get-tuple-element.7, f32[256]{0:T(256)S(1)} %bitcast.5), kind=kLoop, calls=%fused_computation | loop fusion | flops 524288 | bytes 4195328 | tf_op jit(solution)/shard_map/broadcast_in_dim | solution.py:372

commit v2 on v1

--- a/solution.py
+++ b/solution.py
@@ -12,12 +12,31 @@
 CHUNKS = 4
 
 
+STEPS = 256.0
+LIMIT = 32700.0
+HALF = 32768
+TAIL = 8
+
+
 def encode(values, ref, rows):
-    ref[...] = values
+    half = rows // 2
+    peak = jnp.max(jnp.abs(values), axis=0, keepdims=True)
+    code = jnp.ceil(jnp.log(jnp.clip(peak, 1e-35, 3e38)) * STEPS)
+    factor = jnp.exp(code * (-1.0 / STEPS)) * LIMIT
+    whole = jnp.clip(jnp.round(values * factor), -32767.0, 32767.0).astype(jnp.int32)
+    words = whole[0:half] * (2 * HALF) + (whole[half:rows] + HALF)
+    codes = jnp.broadcast_to(code, (TAIL, values.shape[1])).astype(jnp.int32)
+    ref[...] = jnp.concatenate([words, codes], axis=0)
 
 
 def numbers(ref, rows):
-    return ref[...]
+    half = rows // 2
+    message = ref[...]
+    scale = jnp.exp(message[half : half + TAIL].astype(jnp.float32)[0:1, :] * (1.0 / STEPS)) * (1.0 / LIMIT)
+    words = message[0:half]
+    upper = jnp.right_shift(words, 16).astype(jnp.float32)
+    lower = (jnp.bitwise_and(words, 2 * HALF - 1) - HALF).astype(jnp.float32)
+    return jnp.concatenate([upper, lower], axis=0) * scale
 
 
 def kernel(
@@ -337,14 +356,14 @@
         in_specs=[pl.BlockSpec(memory_space=pl.ANY), vmem, smem, smem, smem],
         out_specs=(vmem, vmem),
         scratch_shapes=[
-            pltpu.VMEM((B - 1, piece, width), jnp.float32),
-            pltpu.VMEM((piece, width), jnp.float32),
+            pltpu.VMEM((B - 1, piece // 2 + TAIL, width), jnp.int32),
+            pltpu.VMEM((piece // 2 + TAIL, width), jnp.int32),
             pltpu.VMEM((rows, inner), jnp.bfloat16),
             pltpu.VMEM((B, inner, width), jnp.bfloat16),
-            pltpu.VMEM((B, G - 1, piece, width), jnp.float32),
-            pltpu.VMEM((B, G - 1, piece, width), jnp.float32),
+            pltpu.VMEM((B, G - 1, piece // 2 + TAIL, width), jnp.int32),
+            pltpu.VMEM((B, G - 1, piece // 2 + TAIL, width), jnp.int32),
             pltpu.VMEM((window_blocks, piece, BS), jnp.float32),
-            pltpu.VMEM((B - 1, piece, width), jnp.float32),
+            pltpu.VMEM((B - 1, piece // 2 + TAIL, width), jnp.int32),
             pltpu.VMEM((8, width), jnp.float32),
             pltpu.VMEM((G - 1, 8, width), jnp.float32),
             pltpu.SMEM((window_blocks,), jnp.int32),

time: 162 us -> 124 us (0.77)
  Pallas kernels: 157 us -> 119 us
    pallas_call x1, Pallas kernels: 157 us -> 119 us  [shards(): pl.pallas_call(functools.partial(kernel, G, B), out_shape=(jax.ShapeDtype...]
where the time goes in v2:
time: 124 us
  Pallas kernels  119 us (96%)
  other arithmetic  3.12 us (3%)
  local copies, waits for them, and re-layouts  2.09 us (2%)
    pallas_call x1, Pallas kernels, shards(): pl.pallas_call(functools.partial(kernel, G, B), out_shape=(jax.ShapeDtype...  119 us
    broadcast_in_dim x1, other arithmetic, shards(): return owned[:, None, :, :]  3.12 us

profile of v2, /device:TPU:25, one launch (start us, length us, event | category | flops | bytes accessed | tf_op | source)
XLA Modules:
  0.0 123.8 jit_solution(5239259854187354893)
XLA Ops:
  0.0 1.4 %copy.6.pruned_ref = s32[64,16]{1,0:T(8,128)} copy(s32[64,16]{0,1:T(8,128)} %param.8) | data formatting | bytes 8192 | tf_op args[3]
  1.4 118.5 %expand.1 = (f32[8,256,256]{2,1,0:T(8,128)}, f32[8,256]{1,0:T(8,128)}) custom-call(bf16[1024,2048]{1,0:T(8,128)(2,1)} %matrix_ref.1, bf16[2048,256]{1,0:T(8,128)(2,1)} %panel_ref.1, s32[64,64]{1,0:T(8,128)} %pattern_ref.1, s32[64,16]{1,0:T(8,128)} %copy.6.pruned_ref, s32[16]{0:T(128)} %owners_ref.1), custom_call_target="tpu_custom_call" | custom-call | flops 8589934592 | bytes 8388608 | tf_op jit(solution)/shard_map/expand/pallas_call | solution.py:350
  119.9 0.7 slice.3
  120.6 3.1 %multiply_bitcast_fusion = f32[8,1,256,256]{3,2,1,0:T(8,128)} fusion(f32[8,256,256]{2,1,0:T(8,128)} %get-tuple-element.7, f32[256]{0:T(256)S(1)} %bitcast.5), kind=kLoop, calls=%fused_computation | loop fusion | flops 524288 | bytes 4195328 | tf_op jit(solution)/shard_map/broadcast_in_dim | solution.py:391
